TPU v7x, 32 devices: a whole 2x2x4 slice. The times are simulated.
32 devices in a mesh: seq: 8 (over z, x), ch: 4 (over y, core).
Axes of the slice: x: 2, y: 2, z: 4, core: 2. Of those that a mesh axis runs over, the one named last changes fastest.
Arguments:
- features: bfloat16 [4096, 1024], P('seq', 'ch'), may hold values from -6 to 6
- w_qkv: bfloat16 [1024, 3072], P('ch'), may hold values from -0.1875 to 0.1875
- log_gate: float32 [8, 4096], P(None, ('seq', 'ch')), may hold values from -1 to 0
- norm_gain: float32 [1024], replicated, may hold values from 0.1 to 1.9
- w_pred: bfloat16 [4, 1024, 1024], replicated, may hold values from -0.1875 to 0.1875
- patch_mask: int32 [4096], P(('seq', 'ch')), may hold values 0 or 1
- neg_index: int32 [4, 32], P(None, ('seq', 'ch')), may hold values from 0 to 4095, as said below
Outputs:
- context: bfloat16 [4096, 1024], P(('seq', 'ch'))
- nce_loss: float32 [4, 4096], P(None, ('seq', 'ch'))
Inputs may be any that keep to these rules, and one draw needn't show every extreme that they name: `neg_index`: negative n of every offset lies among the 128 patches of block n, blocks of 128 consecutive patches.
All inputs are finite; a program needn't handle non-finite values. No bound on the sum of `patch_mask` on one device may be relied on, other than what follows from the above.
Results may differ from a plain program's by a relative error of at most 0.0061.
Values may be sent and summed in bfloat16 or wider, within the bound.
A program may use at most 320 MiB of HBM per device.

v0:
```python
import jax
import jax.numpy as jnp
from jax import lax
from jax.sharding import PartitionSpec as P

CIN = 1024
HEADS = 8
HEAD_DIM = 128
K = 4


norm_eps = 1e-06


def prefix(part, axis, combine, identity):
    place = lax.axis_index(axis)
    gathered = jax.tree.map(lambda a: lax.all_gather(a, axis), part)
    state = jax.tree.map(lambda a, e: jnp.zeros_like(a) + jnp.asarray(e, a.dtype), part, identity)

    def one(turn, state):
        return combine(
            state, jax.tree.map(lambda a: lax.dynamic_index_in_dim(a, turn, 0, False), gathered)
        )

    return lax.fori_loop(0, place, one, state)


def shifted(x, axis, by):
    length = lax.axis_size(axis)
    pairs = [(i, i + by) for i in range(length) if 0 <= i + by < length]
    return lax.ppermute(x, axis, pairs)


def combine_states(earlier, later):
    return (earlier[0] * later[0], later[0][:, None, None] * earlier[1] + later[1])


def shards(features, w_qkv, log_gate, norm_gain, w_pred, patch_mask, neg_index):
    groups = lax.axis_size("ch")
    length = features.shape[0] // groups
    row_width = length // 2
    inner = HEADS * HEAD_DIM
    highest = lax.Precision.HIGHEST
    score_scale = 4.0 * CIN ** (-0.5)
    column_block = lax.all_to_all(w_qkv, "ch", split_axis=1, concat_axis=0, tiled=True)
    block_rows = lax.all_gather(features, "ch", axis=1, tiled=True)
    encoded = lax.dynamic_slice_in_dim(block_rows, lax.axis_index("ch") * length, length, 0)
    column_part = jnp.dot(block_rows, column_block, preferred_element_type=jnp.float32).astype(
        jnp.bfloat16
    )
    projected = lax.all_to_all(column_part, "ch", split_axis=0, concat_axis=1, tiled=True)
    mask_wire = patch_mask.astype(jnp.bfloat16)
    maskf = patch_mask.astype(jnp.float32)
    queries = projected[:, :inner].astype(jnp.float32).reshape(length, HEADS, HEAD_DIM)
    keys_local = (
        projected[:, inner : 2 * inner].astype(jnp.float32).reshape(length, HEADS, HEAD_DIM)
    )
    values = (
        (projected[:, 2 * inner :] * mask_wire[:, None])
        .astype(jnp.float32)
        .reshape(length, HEADS, HEAD_DIM)
    )
    cumul = jnp.cumsum(log_gate, axis=1)
    lower = jnp.arange(length)[:, None] >= jnp.arange(length)[None, :]
    scores = jnp.einsum("thd,shd->hts", queries, keys_local, precision=highest)
    diff = cumul[:, :, None] - cumul[:, None, :]
    decay = jnp.where(lower[None], jnp.exp(jnp.where(lower[None], diff, 0.0)), 0.0)
    intra = jnp.einsum("hts,shd->thd", scores * decay, values, precision=highest)
    tail = jnp.exp(cumul[:, -1:] - cumul)
    summary = jnp.einsum("shd,she->hde", keys_local * tail.T[:, :, None], values, precision=highest)
    block_decay = jnp.exp(cumul[:, -1])
    identity = (
        jnp.ones((HEADS,), jnp.float32),
        jnp.zeros((HEADS, HEAD_DIM, HEAD_DIM), jnp.float32),
    )
    incoming = prefix((block_decay, summary), ("seq", "ch"), combine_states, identity)
    inter = (
        jnp.einsum("thd,hde->the", queries, incoming[1], precision=highest)
        * jnp.exp(cumul).T[:, :, None]
    )
    mixed = (intra + inter) * HEAD_DIM ** (-0.5)
    squares = jnp.mean(mixed * mixed, axis=-1, keepdims=True)
    normed = (mixed / jnp.sqrt(squares + norm_eps)).reshape(length, inner)
    context = (normed * norm_gain).astype(jnp.bfloat16)
    predicted = jnp.einsum(
        "td,kdc->ktc", context, w_pred, preferred_element_type=jnp.float32
    ).astype(jnp.bfloat16)
    base_row = lax.axis_index(("seq", "ch")) * length
    local_index = neg_index - base_row
    owned = jnp.take(encoded, local_index, axis=0)
    logits = (
        jnp.einsum(
            "ktc,kjc->ktj",
            predicted,
            lax.all_gather(owned, ("seq", "ch"), axis=1, tiled=True),
            preferred_element_type=jnp.float32,
        )
        * score_scale
    )
    negsum = jnp.sum(jnp.exp(logits), axis=2)
    ahead_rows = [encoded]
    ahead_mask = [mask_wire]
    for distance in (1, 2):
        target_rows, target_flags = shifted((encoded, mask_wire), ("seq", "ch"), -distance)
        ahead_rows.append(target_rows)
        ahead_mask.append(target_flags)
    ahead_rows = jnp.concatenate(ahead_rows, axis=0)
    ahead_mask = jnp.concatenate(ahead_mask, axis=0)
    losses = []
    for offset in range(1, K + 1):
        begin = offset * row_width
        target = ahead_rows[begin : begin + length]
        target_mask = ahead_mask[begin : begin + length]
        positive = (
            jnp.einsum(
                "tc,tc->t", predicted[offset - 1], target, preferred_element_type=jnp.float32
            )
            * score_scale
        )
        valid = maskf * target_mask.astype(jnp.float32)
        losses.append(valid * (jnp.log(jnp.exp(positive) + negsum[offset - 1]) - positive))
    return (context, jnp.stack(losses, axis=0))


def solution(mesh):
    placed = (
        P("seq", "ch"),
        P("ch", None),
        P(None, ("seq", "ch")),
        P(),
        P(),
        P(("seq", "ch")),
        P(None, ("seq", "ch")),
    )
    return jax.shard_map(
        shards,
        mesh=mesh,
        in_specs=placed,
        out_specs=(P(("seq", "ch"), None), P(None, ("seq", "ch"))),
        check_vma=False,
    )
```

profile of v0, /device:TPU:31, one launch (start us, length us, event | category | flops | bytes accessed | tf_op | source)
XLA Modules:
  0.0 230.0 jit_solution(5786956965018925870)
XLA Ops:
  7.2 0.7 all-gather.5.cloned.1.call-update
  7.9 1.7 copy.38
  9.6 27.2 %all_to_all.38 = bf16[256,4,768]{0,2,1:T(8,128)(2,1)S(1)} all-to-all(bf16[256,4,768]{0,2,1:T(8,128)(2,1)S(1)} %bitcast.120), channel_id=1, replica_groups=mesh['seq'=8,'ch'=4] {'ch'}, dimensions={1} | all-to-all | bytes 3145728 | tf_op jit(solution)/shard_map/all_to_all | solution.py:45
  36.8 0.7 copy.39
  37.6 2.2 convolution_convert_fusion.1
  39.8 1.2 copy.40
  41.0 5.3 %all-to-all-start.1 = ((bf16[4,128,768]{1,2,0:T(8,128)(2,1)}), bf16[4,128,768]{1,2,0:T(8,128)(2,1)S(1)}, u32[]{:S(2)}, u32[]{:S(2)}) async-start(bf16[4,128,768]{1,2,0:T(8,128)(2,1)} %copy.40), calls=%async_computation.1 | async-start | bytes 1572864 | tf_op jit(solution)/shard_map/all_to_all | solution.py:51
  46.3 0.3 reduce_window_sum.11
  46.6 0.2 slice_reduce_fusion
  46.9 9.2 %all-to-all-done.1 = bf16[4,128,768]{1,2,0:T(8,128)(2,1)S(1)} async-done(((bf16[4,128,768]{1,2,0:T(8,128)(2,1)}), bf16[4,128,768]{1,2,0:T(8,128)(2,1)S(1)}, u32[]{:S(2)}, u32[]{:S(2)}) %all-to-all-start.1) | async-done | bytes 786464 | tf_op jit(solution)/shard_map/all_to_all | solution.py:51
  56.1 1.5 fusion.10
  57.6 2.5 %collective-permute-start = (bf16[128]{0:T(256)(128)(2,1)S(1)}, bf16[128]{0:T(256)(128)(2,1)S(1)}, u32[]{:S(2)}, u32[]{:S(2)}) collective-permute-start(bf16[128]{0:T(256)(128)(2,1)S(1)} %convert_element_type.34), channel_id=1, source_target_pairs={{1,0},{2,1},{3,2},{4,3},{5,4},{6,5},{7,6},{8,7},{9,8},{10,9},{11,1... | collective-permute-start | bytes 776 | tf_op jit(solution)/shard_map/ppermute | solution.py:31
  60.1 3.3 %collective-permute-start.2 = (bf16[128]{0:T(256)(128)(2,1)S(1)}, bf16[128]{0:T(256)(128)(2,1)S(1)}, u32[]{:S(2)}, u32[]{:S(2)}) collective-permute-start(bf16[128]{0:T(256)(128)(2,1)S(1)} %convert_element_type.34), channel_id=1, source_target_pairs={{2,0},{3,1},{4,2},{5,3},{6,4},{7,5},{8,6},{9,7},{10,8},{11,9},{12,... | collective-permute-start | bytes 776 | tf_op jit(solution)/shard_map/ppermute | solution.py:31
  63.5 0.2 dynamic-update-slice
  63.7 40.0 %all-reduce = f32[256]{0:T(256)S(1)} all-reduce(f32[256]{0:T(256)S(1)} %dynamic-update-slice), channel_id=2, replica_groups=mesh['seq'=8,'ch'=4] {'seq','ch'}, use_global_device_ids=true, to_apply=%add | all-reduce | flops 256 | bytes 2048
  103.7 0.1 reshape.118
  103.9 1.0 constant_dynamic-slice_fusion
  104.8 3.0 %collective-permute-start.1 = (bf16[128,1024]{1,0:T(8,128)(2,1)S(1)}, bf16[128,1024]{1,0:T(8,128)(2,1)S(1)}, u32[]{:S(2)}, u32[]{:S(2)}) collective-permute-start(bf16[128,1024]{1,0:T(8,128)(2,1)S(1)} %constant_dynamic-slice_fusion), channel_id=1, source_target_pairs={{1,0},{2,1},{3,2},{4,3},{5,4},{6,5},{7,6},{8,7},{9,8},{10,9},{11,1... | collective-permute-start | bytes 786440 | tf_op jit(solution)/shard_map/ppermute | solution.py:31
  107.9 3.5 %collective-permute-start.3 = (bf16[128,1024]{1,0:T(8,128)(2,1)S(1)}, bf16[128,1024]{1,0:T(8,128)(2,1)S(1)}, u32[]{:S(2)}, u32[]{:S(2)}) collective-permute-start(bf16[128,1024]{1,0:T(8,128)(2,1)S(1)} %constant_dynamic-slice_fusion), channel_id=1, source_target_pairs={{2,0},{3,1},{4,2},{5,3},{6,4},{7,5},{8,6},{9,7},{10,8},{11,9},{12,... | collective-permute-start | bytes 786440 | tf_op jit(solution)/shard_map/ppermute | solution.py:31
  111.4 0.6 gather_fusion
  111.9 0.1 bitcast_select_fusion
  112.0 37.9 %all_gather.20 = bf16[4,32,1024]{2,0,1:T(4,128)(2,1)S(1)} all-gather(bf16[4,1,1024]{2,0,1:T(4,128)(2,1)S(1)} %bitcast_select_fusion), channel_id=1, replica_groups=mesh['seq'=8,'ch'=4] {'seq','ch'}, dimensions={1}, use_global_device_ids=true | all-gather | bytes 270336 | tf_op jit(solution)/shard_map/all_gather | solution.py:95
  149.9 0.3 convolution_multiply_fusion
  150.2 26.6 %all-gather.7.cloned.1.call-done = f32[256,128,128]{2,1,0:T(8,128)} async-done(((f32[8,128,128]{2,1,0:T(8,128)}), f32[256,128,128]{2,1,0:T(8,128)}) %all-gather.7.cloned.1.call-update) | async-done | bytes 16777232 | tf_op jit(solution)/shard_map/all_gather | solution.py:17
  176.8 38.4 %while.12 = (s32[]{:T(128)}, f32[8,128,128]{2,1,0:T(8,128)S(1)}, s32[]{:T(128)}, f32[32,8]{1,0:T(8,128)S(1)}, f32[32,8,128,128]{3,2,1,0:T(8,128)}, /*index=5*/s32[]{:T(128)}, s32[]{:T(128)}, s32[]{:T(128)}) while((s32[]{:T(128)}, f32[8,128,128]{2,1,0:T(8,128)S(1)}, s32[]{:T(128)}, f32[32,8]{1,0:T(8,128)S(1)}, f32[32,8,128,128]{3,2,1,0:T(8,128)}, ...), condition=%wide.region_2.3_spmd, body=%wide.region_1.2_spmd.sunk | while | flops 262149 | bytes 1573087 | solution.py:25
  176.9 1.2 bitcast_add_fusion.6
  178.1 1.2 bitcast_add_fusion.6
  179.4 1.2 bitcast_add_fusion.6
  180.6 1.2 bitcast_add_fusion.6
  181.8 1.2 bitcast_add_fusion.6
  183.1 1.2 bitcast_add_fusion.6
  184.3 1.2 bitcast_add_fusion.6
  185.5 1.2 bitcast_add_fusion.6
  186.8 1.2 bitcast_add_fusion.6
  188.0 1.2 bitcast_add_fusion.6
  189.3 1.2 bitcast_add_fusion.6
  190.5 1.2 bitcast_add_fusion.6
  191.7 1.2 bitcast_add_fusion.6
  193.0 1.2 bitcast_add_fusion.6
  194.2 1.2 bitcast_add_fusion.6
  195.4 1.2 bitcast_add_fusion.6
  196.7 1.2 bitcast_add_fusion.6
  197.9 1.2 bitcast_add_fusion.6
  199.2 1.2 bitcast_add_fusion.6
  200.4 1.2 bitcast_add_fusion.6
  201.6 1.2 bitcast_add_fusion.6
  202.9 1.2 bitcast_add_fusion.6
  204.1 1.2 bitcast_add_fusion.6
  205.3 1.2 bitcast_add_fusion.6
  206.6 1.2 bitcast_add_fusion.6
  207.8 1.2 bitcast_add_fusion.6
  209.1 1.2 bitcast_add_fusion.6
  210.3 1.2 bitcast_add_fusion.6
  211.5 1.2 bitcast_add_fusion.6
  212.8 1.2 bitcast_add_fusion.6
  214.0 1.2 bitcast_add_fusion.6
  215.2 0.6 fusion.3
  215.8 0.7 multiply_reduce_fusion
  216.6 0.2 copy.46
  216.9 4.7 %fusion = bf16[4,128,1024]{2,1,0:T(8,128)(2,1)S(1)} fusion(bf16[4,1024,1024]{2,1,0:T(8,128)(2,1)} %param.13, bf16[128,1024]{1,0:T(8,128)(2,1)S(1)} %multiply_convert_fusion), kind=kOutput, calls=%fused_computation.5 | convolution fusion | flops 1074266112 | bytes 9699328 | tf_op jit(solution)/shard_map/td,kdc->ktc/dot_general | solution.py:85
  221.6 0.5 fusion.5
  222.2 0.4 fusion.9
  222.5 0.1 fusion.28
  222.6 0.6 pad_maximum_fusion.2
  (61 shorter events, 0.8 us)
Async XLA Ops:
  7.2 30.4 %all-gather.5.cloned.1.call-start = ((), (), s32[]{:S(2)}) async-start(), calls=%async_computation.2 | async-start | bytes 1310720 | tf_op jit(solution)/shard_map/all_gather | solution.py:46
  39.8 6.5 %copy-start.3 = (s32[128]{0:T(128)S(1)}, s32[128]{0:T(128)}, u32[]{:S(2)}) copy-start(s32[128]{0:T(128)} %param.14) | copy-start | bytes 1540
  39.8 6.5 %copy-start.2 = (f32[8,128]{1,0:T(8,128)S(1)}, f32[8,128]{1,0:T(8,128)}, u32[]{:S(2)}) copy-start(f32[8,128]{1,0:T(8,128)} %param.11) | copy-start | bytes 12292
  41.0 15.1 %all-to-all-start.1 = ((bf16[4,128,768]{1,2,0:T(8,128)(2,1)}), bf16[4,128,768]{1,2,0:T(8,128)(2,1)S(1)}, u32[]{:S(2)}, u32[]{:S(2)}) async-start(bf16[4,128,768]{1,2,0:T(8,128)(2,1)} %copy.40), calls=%async_computation.1 | async-start | bytes 1572864 | tf_op jit(solution)/shard_map/all_to_all | solution.py:51
  46.3 130.5 %all-gather.7.cloned.1.call-start = ((), (), s32[]{:S(2)}) async-start(), calls=%async_computation.3 | async-start | bytes 17301504 | tf_op jit(solution)/shard_map/all_gather | solution.py:17
  56.1 47.7 %copy-start.4 = (s32[4,1]{0,1:T(1,128)S(1)}, s32[4,1]{0,1:T(1,128)}, u32[]{:S(2)}) copy-start(s32[4,1]{0,1:T(1,128)} %param.15) | copy-start | bytes 52
  57.6 46.2 %collective-permute-start = (bf16[128]{0:T(256)(128)(2,1)S(1)}, bf16[128]{0:T(256)(128)(2,1)S(1)}, u32[]{:S(2)}, u32[]{:S(2)}) collective-permute-start(bf16[128]{0:T(256)(128)(2,1)S(1)} %convert_element_type.34), channel_id=1, source_target_pairs={{1,0},{2,1},{3,2},{4,3},{5,4},{6,5},{7,6},{8,7},{9,8},{10,9},{11,1... | collective-permute-start | bytes 776 | tf_op jit(solution)/shard_map/ppermute | solution.py:31
  60.1 43.7 %collective-permute-start.2 = (bf16[128]{0:T(256)(128)(2,1)S(1)}, bf16[128]{0:T(256)(128)(2,1)S(1)}, u32[]{:S(2)}, u32[]{:S(2)}) collective-permute-start(bf16[128]{0:T(256)(128)(2,1)S(1)} %convert_element_type.34), channel_id=1, source_target_pairs={{2,0},{3,1},{4,2},{5,3},{6,4},{7,5},{8,6},{9,7},{10,8},{11,9},{12,... | collective-permute-start | bytes 776 | tf_op jit(solution)/shard_map/ppermute | solution.py:31
  104.8 117.3 %collective-permute-start.1 = (bf16[128,1024]{1,0:T(8,128)(2,1)S(1)}, bf16[128,1024]{1,0:T(8,128)(2,1)S(1)}, u32[]{:S(2)}, u32[]{:S(2)}) collective-permute-start(bf16[128,1024]{1,0:T(8,128)(2,1)S(1)} %constant_dynamic-slice_fusion), channel_id=1, source_target_pairs={{1,0},{2,1},{3,2},{4,3},{5,4},{6,5},{7,6},{8,7},{9,8},{10,9},{11,1... | collective-permute-start | bytes 786440 | tf_op jit(solution)/shard_map/ppermute | solution.py:31
  107.9 114.3 %collective-permute-start.3 = (bf16[128,1024]{1,0:T(8,128)(2,1)S(1)}, bf16[128,1024]{1,0:T(8,128)(2,1)S(1)}, u32[]{:S(2)}, u32[]{:S(2)}) collective-permute-start(bf16[128,1024]{1,0:T(8,128)(2,1)S(1)} %constant_dynamic-slice_fusion), channel_id=1, source_target_pairs={{2,0},{3,1},{4,2},{5,3},{6,4},{7,5},{8,6},{9,7},{10,8},{11,9},{12,... | collective-permute-start | bytes 786440 | tf_op jit(solution)/shard_map/ppermute | solution.py:31
  215.8 1.0 copy-start.1
  216.9 4.8 %copy-start = (bf16[128,1024]{1,0:T(8,128)(2,1)}, bf16[128,1024]{1,0:T(8,128)(2,1)S(1)}, u32[]{:S(2)}) copy-start(bf16[128,1024]{1,0:T(8,128)(2,1)S(1)} %multiply_convert_fusion) | copy-start | bytes 786436
Sparse Core Ops, SparseCore 0:
  9.5 22.9 all-gather.4
  57.7 119.0 all-gather.6
where the time goes:
time: 232 us; the launch traced here: 230 us
  blocking collectives  105 us (45%)
  other arithmetic  38.5 us (17%)
  waiting for transfers between devices  36.5 us (16%)
  starting transfers between devices  17.7 us (8%)
  between operations  14.3 us (6%)
  matrix products  10.5 us (5%)
  local copies, waits for them, and re-layouts  6.25 us (3%)
    unnamed x1, blocking collectives  40 us
    all_gather x1, blocking collectives, shards(): lax.all_gather(owned, ('seq', 'ch'), axis=1, tiled=True)  37.9 us
    add x31, other arithmetic, combine_states(): later[0][:, None, None] * earlier[1] + later[1]  36.9 us
    all_to_all x1, blocking collectives, shards(): lax.all_to_all(w_qkv, 'ch', split_axis=1, concat_axis=0, tiled=True)  27.2 us
    all_gather x1, waiting for transfers between devices, prefix(): gathered = jax.tree.map(lambda a: lax.all_gather(a, axis), part)  26.6 us
    ppermute x4, starting transfers between devices, shifted(): return lax.ppermute(x, axis, pairs)  12.3 us
    all_to_all x1, waiting for transfers between devices, shards(): lax.all_to_all(column_part, 'ch', split_axis=0, concat_axis=1, tiled=True)  9.19 us
    all_to_all x1, starting transfers between devices, shards(): lax.all_to_all(column_part, 'ch', split_axis=0, concat_axis=1, tiled=True)  5.35 us
  transfers between devices with their start and end apart: 7, of which 2 were waited for; matrix products, arithmetic and copies ran while one was open for 21% of the time, Pallas kernels for 0%

commit v1 on v0

v1 whole, which is shorter than its diff:
```python
import functools

import jax
import jax.numpy as jnp
from jax import lax
from jax.experimental import pallas as pl
from jax.experimental.pallas import tpu as pltpu
from jax.sharding import PartitionSpec as P

HEADS = 8
HEAD_DIM = 128
K = 4
MASK_ROW = 8
NEG_ROW = 9
AUX_ROWS = 16
MESH = pl.DeviceIdType.MESH
norm_eps = 1e-06
highest = lax.Precision.HIGHEST
across = (((1,), (1,)), ((), ()))
down = (((0,), (0,)), ((), ()))


def dot(a, b, dims=(((1,), (0,)), ((), ())), precision=None):
    return lax.dot_general(a, b, dims, precision=precision, preferred_element_type=jnp.float32)


def split(x):
    high = x.astype(jnp.bfloat16)
    return high, (x - high.astype(jnp.float32)).astype(jnp.bfloat16)


def kernel(
    S, C,
    feat_hbm, w_hbm, gate_ref, gain_ref, wpred_hbm, mask_ref, neg_ref,
    ctx_ref, loss_ref,
    feat_all, w_all, aux_all, sel, totals, bank, proj, qkv, cumrow, cumcol,
    state_out, state_in, carried, ctx_out, ctx_in, wpred,
    local_sem, ch_send, ch_recv, tot_send, tot_recv, bank_send, bank_recv,
    ext_send, ext_recv, st_send, st_recv, ctx_send, ctx_recv,
):
    L = gate_ref.shape[1]
    B = C * L
    CB = feat_hbm.shape[1]
    W = qkv.shape[2]
    inner = HEADS * HEAD_DIM
    own_heads = W // HEAD_DIM
    row_width = L // 2
    score_scale = 4.0 * (C * CB) ** (-0.5)
    s, c = lax.axis_index("seq"), lax.axis_index("ch")

    own = [pltpu.make_async_copy(feat_hbm, feat_all.at[c, pl.ds(0, B)], local_sem.at[0])]
    for p in range(3):
        begin = pl.multiple_of(p * inner + c * W, 128)
        own.append(
            pltpu.make_async_copy(w_hbm.at[:, pl.ds(begin, W)], w_all.at[c, p], local_sem.at[1 + p])
        )
    own.append(pltpu.make_async_copy(wpred_hbm, wpred, local_sem.at[4]))
    for copy in own:
        copy.start()

    aux_all[c, 0:HEADS] = gate_ref[...]
    base = (s * C + c) * L
    local_index = (neg_ref[...] - base).astype(jnp.float32)
    lead = jnp.where(
        lax.broadcasted_iota(jnp.int32, (HEADS, L), 0) == 0,
        jnp.broadcast_to(mask_ref[...].astype(jnp.float32), (HEADS, L)),
        0.0,
    )
    aux_all[c, HEADS:AUX_ROWS] = lead
    aux_all[c, NEG_ROW : NEG_ROW + K] = jnp.broadcast_to(local_index, (K, L))

    barrier = pltpu.get_barrier_semaphore()
    for d in range(1, C):
        pl.semaphore_signal(
            barrier, inc=1, device_id=(s, lax.rem(c + d, C)), device_id_type=MESH
        )
    for d in range(1, S):
        pl.semaphore_signal(
            barrier, inc=1, device_id=(lax.rem(s + d, S), c), device_id_type=MESH
        )
    pl.semaphore_wait(barrier, S + C - 2)

    def to_ch(d, kind):
        peer = lax.rem(c + d, C)
        if kind == 0:
            source, target = aux_all.at[c], aux_all.at[c]
        elif kind == 1:
            source, target = feat_hbm, feat_all.at[c, pl.ds(0, B)]
        else:
            begin = pl.multiple_of((kind - 2) * inner + peer * W, 128)
            source, target = w_hbm.at[:, pl.ds(begin, W)], w_all.at[c, kind - 2]
        return pltpu.make_async_remote_copy(
            source, target, ch_send.at[d - 1, kind], ch_recv.at[d - 1, kind],
            device_id=(s, peer), device_id_type=MESH,
        )

    def to_seq(source, target, sends, recvs, d):
        return pltpu.make_async_remote_copy(
            source, target, sends.at[d - 1], recvs.at[d - 1],
            device_id=(lax.rem(s + d, S), c), device_id_type=MESH,
        )

    sent = [to_ch(d, kind) for kind in range(5) for d in range(1, C)]
    for copy in sent:
        copy.start()
    for d in range(1, C):
        to_ch(d, 0).wait_recv()

    row_id = lax.broadcasted_iota(jnp.int32, (L, L), 0)
    column_id = lax.broadcasted_iota(jnp.int32, (L, L), 1)
    lower = row_id >= column_id
    tril = lower.astype(jnp.float32)
    triu = (row_id <= column_id).astype(jnp.float32)
    sel[...] = jnp.zeros_like(sel)
    row_carry = jnp.zeros((8, 1), jnp.float32)
    column_carry = jnp.zeros((1, 8), jnp.float32)
    for b in range(C):
        for i in range(own_heads):
            sel[b, i : i + 1] = aux_all[b, pl.ds(c * own_heads + i, 1), :]
        gates = sel[b]
        by_row = dot(gates, triu, precision=highest) + row_carry
        by_column = dot(tril, gates, across, precision=highest) + column_carry
        cumrow[:, b * L : (b + 1) * L] = by_row
        cumcol[b * L : (b + 1) * L, :] = by_column
        row_carry = by_row[:, L - 1 : L]
        column_carry = by_column[L - 1 : L, :]
    totals[s] = jnp.broadcast_to(row_carry, (8, 128))
    tot_copies = [to_seq(totals.at[s], totals.at[s], tot_send, tot_recv, d) for d in range(1, S)]
    for copy in tot_copies:
        copy.start()

    own[0].wait()
    for d in range(1, C):
        to_ch(d, 1).wait_recv()

    wanted = jnp.concatenate([aux_all[b, NEG_ROW : NEG_ROW + K, :] for b in range(C)], axis=0)
    negatives = K * C
    owner = lax.broadcasted_iota(jnp.int32, (negatives, L), 0) // K
    lane = lax.broadcasted_iota(jnp.int32, (negatives, L), 1).astype(jnp.float32)
    hit = wanted == lane
    chosen = jnp.concatenate(
        [jnp.where(hit & (owner == b), 1.0, 0.0) for b in range(C)], axis=1
    ).astype(jnp.bfloat16)
    for b in range(C):
        bank[s, b] = dot(chosen, feat_all[b, 0:B, :]).astype(jnp.bfloat16)
    bank_copies = [to_seq(bank.at[s], bank.at[s], bank_send, bank_recv, d) for d in range(1, S)]
    for copy in bank_copies:
        copy.start()

    def ext(kind):
        if kind == 0:
            source, target = feat_all.at[:, pl.ds(0, 2 * L)], feat_all.at[:, pl.ds(B, 2 * L)]
        else:
            source, target = aux_all.at[pl.ds(0, 2)], aux_all.at[pl.ds(C, 2)]
        return pltpu.make_async_remote_copy(
            source, target, ext_send.at[kind], ext_recv.at[kind],
            device_id=(lax.rem(s + S - 1, S), c), device_id_type=MESH,
        )

    reaching = c >= C - 2

    @pl.when(reaching & (s > 0))
    def _():
        ext(0).start()
        ext(1).start()

    @pl.when(s == S - 1)
    def _():
        feat_all[:, B : B + 2 * L, :] = jnp.zeros((C, 2 * L, CB), jnp.bfloat16)
        aux_all[C : C + 2] = jnp.zeros((2, AUX_ROWS, 128), jnp.float32)

    for d in range(C):
        block = lax.rem(c + C - d, C)
        for p in range(3):
            if d == 0:
                own[1 + p].wait()
            else:
                to_ch(d, 2 + p).wait_recv()
            part = dot(feat_all[block, 0:B, :], w_all[block, p])
            if d == 0:
                proj[p] = part
            elif d < C - 1:
                proj[p] = proj[p] + part
            else:
                qkv[p] = (proj[p] + part).astype(jnp.bfloat16)
    eye = (row_id == column_id).astype(jnp.bfloat16)
    for b in range(C):
        keep = dot(eye, aux_all[b].astype(jnp.bfloat16), across)[:, MASK_ROW : MASK_ROW + 1]
        rows = slice(b * L, (b + 1) * L)
        qkv[2, rows, :] = (qkv[2, rows, :].astype(jnp.float32) * keep).astype(jnp.bfloat16)

    for i in range(own_heads):
        head = slice(i * HEAD_DIM, (i + 1) * HEAD_DIM)
        tail = jnp.exp(cumcol[B - 1 : B, i : i + 1] - cumcol[:, i : i + 1])
        high, low = split(qkv[1, :, head].astype(jnp.float32) * tail)
        values = qkv[2, :, head]
        state_out[head, :] = (dot(high, values, down) + dot(low, values, down)).astype(jnp.bfloat16)

    def state_copy(d):
        return to_seq(state_out, state_in.at[s], st_send, st_recv, d)

    for d in reversed(range(1, S)):
        @pl.when(s + d < S)
        def _(d=d):
            state_copy(d).start()

    for i in range(own_heads):
        head = slice(i * HEAD_DIM, (i + 1) * HEAD_DIM)
        for b in range(C):
            rows = slice(b * L, (b + 1) * L)
            width = (b + 1) * L
            scores = dot(qkv[0, rows, head], qkv[1, 0:width, head], across)
            diff = cumcol[rows, i : i + 1] - cumrow[i : i + 1, 0:width]
            seen = (
                lax.broadcasted_iota(jnp.int32, (L, width), 0) + b * L
                >= lax.broadcasted_iota(jnp.int32, (L, width), 1)
            )
            decay = jnp.where(seen, jnp.exp(jnp.where(seen, diff, 0.0)), 0.0)
            high, low = split(scores * decay)
            values = qkv[2, 0:width, head]
            proj[0, rows, head] = dot(high, values) + dot(low, values)

    for d in range(1, S):
        to_seq(totals.at[s], totals.at[s], tot_send, tot_recv, d).wait_recv()
    carried[...] = jnp.zeros_like(carried)

    def absorb(turn, _):
        far = s - turn
        pltpu.make_async_remote_copy(
            state_out, state_in.at[turn], st_send.at[far - 1], st_recv.at[far - 1],
            device_id=(lax.rem(s + 1, S), c), device_id_type=MESH,
        ).wait_recv()
        total = totals[turn]
        for i in range(own_heads):
            head = slice(i * HEAD_DIM, (i + 1) * HEAD_DIM)
            carried[head, :] = (
                jnp.exp(total[i : i + 1, :]) * carried[head, :]
                + state_in[turn, head, :].astype(jnp.float32)
            )
        return 0

    lax.fori_loop(0, s, absorb, 0)

    for i in range(own_heads):
        head = slice(i * HEAD_DIM, (i + 1) * HEAD_DIM)
        high, low = split(carried[head, :])
        gain = gain_ref[pl.ds(c * own_heads + i, 1), :]
        for b in range(C):
            rows = slice(b * L, (b + 1) * L)
            queries = qkv[0, rows, head]
            inter = (dot(queries, high) + dot(queries, low)) * jnp.exp(cumcol[rows, i : i + 1])
            mixed = (proj[0, rows, head] + inter) * HEAD_DIM ** (-0.5)
            squares = jnp.mean(mixed * mixed, axis=-1, keepdims=True)
            normed = mixed / jnp.sqrt(squares + norm_eps)
            ctx_out[b, :, head] = (normed * gain).astype(jnp.bfloat16)

    def to_owner(d):
        peer = lax.rem(c + d, C)
        return pltpu.make_async_remote_copy(
            ctx_out.at[peer], ctx_in.at[c], ctx_send.at[d - 1], ctx_recv.at[d - 1],
            device_id=(s, peer), device_id_type=MESH,
        )

    for d in range(1, C):
        to_owner(d).start()
    ctx_in[c] = ctx_out[c]
    own[4].wait()
    for d in range(1, S):
        to_seq(bank.at[s], bank.at[s], bank_send, bank_recv, d).wait_recv()

    @pl.when(reaching & (s < S - 1))
    def _():
        ext(0).wait_recv()
        ext(1).wait_recv()

    for d in range(1, C):
        to_owner(d).wait_recv()
    for b in range(C):
        ctx_ref[:, b * W : (b + 1) * W] = ctx_in[b]
    context = ctx_ref[...]
    width = S * negatives
    mine = lax.rem(lax.broadcasted_iota(jnp.int32, (L, width), 1), K)
    lanes = lax.broadcasted_iota(jnp.int32, (L, 128), 1)
    positives = jnp.zeros((L, 128), jnp.float32)
    negsums = jnp.zeros((L, 128), jnp.float32)
    for j in range(K):
        predicted = dot(context, wpred[j]).astype(jnp.bfloat16)
        begin = pl.multiple_of(c * L + (j + 1) * row_width, row_width)
        products = jnp.zeros((L, CB), jnp.float32)
        logits = jnp.zeros((L, width), jnp.float32)
        for b in range(C):
            part = predicted[:, b * CB : (b + 1) * CB]
            target = feat_all[b, pl.ds(begin, L), :]
            products = products + part.astype(jnp.float32) * target.astype(jnp.float32)
            logits = logits + dot(part, bank[:, b].reshape(width, CB), across)
        positive = jnp.sum(products, axis=1, keepdims=True) * score_scale
        negsum = jnp.sum(
            jnp.where(mine == j, jnp.exp(logits * score_scale), 0.0), axis=1, keepdims=True
        )
        positives = jnp.where(lanes == j, positive, positives)
        negsums = jnp.where(lanes == j, negsum, negsums)
    positives = positives.T[0:8]
    negsums = negsums.T[0:8]
    losses = jnp.log(jnp.exp(positives) + negsums) - positives
    maskf = aux_all[c, MASK_ROW : MASK_ROW + 1, :]
    for j in range(K):
        first = aux_all[c + (j + 1) // 2, MASK_ROW : MASK_ROW + 1, :]
        if (j + 1) % 2:
            second = aux_all[c + (j + 2) // 2, MASK_ROW : MASK_ROW + 1, :]
            first = jnp.concatenate([first[:, row_width:], second[:, :row_width]], axis=1)
        loss_ref[j : j + 1, :] = maskf * first * losses[j : j + 1]

    for copy in sent + tot_copies + bank_copies:
        copy.wait_send()

    @pl.when(reaching & (s > 0))
    def _():
        ext(0).wait_send()
        ext(1).wait_send()

    for d in range(1, S):
        @pl.when(s + d < S)
        def _(d=d):
            state_copy(d).wait_send()
    for d in range(1, C):
        to_owner(d).wait_send()


def shards(S, C, features, w_qkv, log_gate, norm_gain, w_pred, patch_mask, neg_index):
    B, CB = features.shape
    L = B // C
    W = HEADS * HEAD_DIM // C
    inner = HEADS * HEAD_DIM
    vmem = pl.BlockSpec(memory_space=pltpu.VMEM)
    hbm = pl.BlockSpec(memory_space=pl.ANY)
    bf16, f32 = jnp.bfloat16, jnp.float32
    dma = pltpu.SemaphoreType.DMA
    return pl.pallas_call(
        functools.partial(kernel, S, C),
        out_shape=(
            jax.ShapeDtypeStruct((L, inner), bf16),
            jax.ShapeDtypeStruct((K, L), f32),
        ),
        in_specs=[hbm, hbm, vmem, vmem, hbm, vmem, vmem],
        out_specs=(vmem, vmem),
        scratch_shapes=[
            pltpu.VMEM((C, B + 2 * L, CB), bf16),
            pltpu.VMEM((C, 3, CB, W), bf16),
            pltpu.VMEM((C + 2, AUX_ROWS, 128), f32),
            pltpu.VMEM((C, 8, 128), f32),
            pltpu.VMEM((S, 8, 128), f32),
            pltpu.VMEM((S, C, K * C, CB), bf16),
            pltpu.VMEM((3, B, W), f32),
            pltpu.VMEM((3, B, W), bf16),
            pltpu.VMEM((8, B), f32),
            pltpu.VMEM((B, 8), f32),
            pltpu.VMEM((W, HEAD_DIM), bf16),
            pltpu.VMEM((S, W, HEAD_DIM), bf16),
            pltpu.VMEM((W, HEAD_DIM), f32),
            pltpu.VMEM((C, L, W), bf16),
            pltpu.VMEM((C, L, W), bf16),
            pltpu.VMEM(w_pred.shape, bf16),
            dma((5,)),
            dma((C - 1, 5)),
            dma((C - 1, 5)),
            dma((S - 1,)),
            dma((S - 1,)),
            dma((S - 1,)),
            dma((S - 1,)),
            dma((2,)),
            dma((2,)),
            dma((S - 1,)),
            dma((S - 1,)),
            dma((C - 1,)),
            dma((C - 1,)),
        ],
        compiler_params=pltpu.CompilerParams(
            collective_id=0, has_side_effects=True, vmem_limit_bytes=48 * 2**20
        ),
    )(
        features,
        w_qkv,
        log_gate,
        norm_gain.reshape(HEADS, HEAD_DIM),
        w_pred,
        patch_mask.reshape(1, L),
        neg_index,
    )


def solution(mesh):
    placed = (
        P("seq", "ch"),
        P("ch", None),
        P(None, ("seq", "ch")),
        P(),
        P(),
        P(("seq", "ch")),
        P(None, ("seq", "ch")),
    )
    return jax.shard_map(
        functools.partial(shards, mesh.shape["seq"], mesh.shape["ch"]),
        mesh=mesh,
        in_specs=placed,
        out_specs=(P(("seq", "ch"), None), P(None, ("seq", "ch"))),
        check_vma=False,
    )
```

time: 232 us -> 62.4 us (0.27)
  the two profiles are of different devices: /device:TPU:31 before, /device:TPU:21 now
where the time goes in v1:
time: 62.4 us; the launch traced here: 62.1 us
  Pallas kernels  55.1 us (88%)
  local copies, waits for them, and re-layouts  6.41 us (10%)
  between operations  0.64 us (1%)
    pallas_call x1, Pallas kernels, shards(): pl.pallas_call(functools.partial(kernel, S, C), out_shape=(jax.ShapeDtype...  55.1 us
    unnamed x13, local copies, waits for them, and re-layouts  6.41 us

profile of v1, /device:TPU:21, one launch (start us, length us, event | category | flops | bytes accessed | tf_op | source)
XLA Modules:
  0.0 62.1 jit_solution(3396608377675366945)
XLA Ops:
  0.6 0.7 %copy.9.neg_ref = s32[4,1]{1,0:T(4,128)S(1)} copy(s32[4,1]{0,1:T(1,128)} %param.13) | data formatting | bytes 32 | tf_op args[6]
  1.4 0.0 copy-start
  1.4 1.4 %copy-done = bf16[256,3072]{1,0:T(8,128)(2,1)S(1)} copy-done((bf16[256,3072]{1,0:T(8,128)(2,1)S(1)}, bf16[256,3072]{1,0:T(8,128)(2,1)}, u32[]{:S(2)}) %copy-start) | copy-done | bytes 1572888
  2.8 0.0 copy-start.1
  2.8 0.9 %copy-done.1 = bf16[512,256]{1,0:T(8,128)(2,1)S(1)} copy-done((bf16[512,256]{1,0:T(8,128)(2,1)S(1)}, bf16[512,256]{1,0:T(8,128)(2,1)}, u32[]{:S(2)}) %copy-start.1) | copy-done | bytes 262168
  3.7 0.0 copy-start.2
  3.7 0.7 %copy-done.2 = f32[8,128]{1,0:T(8,128)S(1)} copy-done((f32[8,128]{1,0:T(8,128)S(1)}, f32[8,128]{1,0:T(8,128)}, u32[]{:S(2)}) %copy-start.2) | copy-done | bytes 4120
  4.4 0.0 copy-start.3
  4.4 0.7 %copy-done.3 = f32[1024]{0:T(1024)S(1)} copy-done((f32[1024]{0:T(1024)S(1)}, f32[1024]{0:T(1024)}, u32[]{:S(2)}) %copy-start.3) | copy-done | bytes 4120
  5.1 0.0 copy-start.4
  5.1 0.7 %copy-done.4 = s32[128]{0:T(128)S(1)} copy-done((s32[128]{0:T(128)S(1)}, s32[128]{0:T(128)}, u32[]{:S(2)}) %copy-start.4) | copy-done | bytes 536
  5.8 55.1 %shard_map.86 = (bf16[128,1024]{1,0:T(8,128)(2,1)S(1)}, f32[4,128]{1,0:T(4,128)S(1)}) custom-call(bf16[512,256]{1,0:T(8,128)(2,1)S(1)} %copy-done.1, bf16[256,3072]{1,0:T(8,128)(2,1)S(1)} %copy-done, f32[8,128]{1,0:T(8,128)S(1)} %copy-done.2, f32[8,128]{1,0:T(8,128)S(1)} %bitcast.2, bf16[4,1024,1024]{2,1,0:T(8,128)(2,1)} %wpred_hbm.1, s32[1,128]{1,0:T(1,128)S(1)} %bitcast.3, ...), custom_call_target="tpu_custom_call" | custom-call | tf_op jit(solution)/shard_map/pallas_call | solution.py:338
  60.8 0.7 %copy.12 = bf16[128,1024]{1,0:T(8,128)(2,1)} copy(bf16[128,1024]{1,0:T(8,128)(2,1)S(1)} %get-tuple-element.4) | data formatting | bytes 524288
  61.5 0.6 copy.13
Async XLA Ops:
  1.4 1.4 %copy-start = (bf16[256,3072]{1,0:T(8,128)(2,1)S(1)}, bf16[256,3072]{1,0:T(8,128)(2,1)}, u32[]{:S(2)}) copy-start(bf16[256,3072]{1,0:T(8,128)(2,1)} %w_hbm.1) | copy-start | bytes 4718596
  2.8 0.9 %copy-start.1 = (bf16[512,256]{1,0:T(8,128)(2,1)S(1)}, bf16[512,256]{1,0:T(8,128)(2,1)}, u32[]{:S(2)}) copy-start(bf16[512,256]{1,0:T(8,128)(2,1)} %feat_hbm.1) | copy-start | bytes 786436
  3.7 0.7 %copy-start.2 = (f32[8,128]{1,0:T(8,128)S(1)}, f32[8,128]{1,0:T(8,128)}, u32[]{:S(2)}) copy-start(f32[8,128]{1,0:T(8,128)} %gate_ref.1) | copy-start | bytes 12292
  4.4 0.7 %copy-start.3 = (f32[1024]{0:T(1024)S(1)}, f32[1024]{0:T(1024)}, u32[]{:S(2)}) copy-start(f32[1024]{0:T(1024)} %param.10) | copy-start | bytes 12292
  5.1 0.7 %copy-start.4 = (s32[128]{0:T(128)S(1)}, s32[128]{0:T(128)}, u32[]{:S(2)}) copy-start(s32[128]{0:T(128)} %param.12) | copy-start | bytes 1540

commit v2 on v1

--- a/solution.py
+++ b/solution.py
@@ -31,11 +31,13 @@
 
 def kernel(
     S, C,
-    feat_hbm, w_hbm, gate_ref, gain_ref, wpred_hbm, mask_ref, neg_ref,
+    feat_hbm, w_hbm, gate_hbm, gain_hbm, wpred_hbm, mask_hbm, neg_hbm,
     ctx_ref, loss_ref,
+    gate_ref, gain_ref, mask_ref, neg_ref,
     feat_all, w_all, aux_all, sel, totals, bank, proj, qkv, cumrow, cumcol,
     state_out, state_in, carried, ctx_out, ctx_in, wpred,
-    local_sem, ch_send, ch_recv, tot_send, tot_recv, bank_send, bank_recv,
+    small_sem, local_sem, ch_send, ch_recv, feat_send, feat_recv, pass_send, pass_recv,
+    w_send, w_recv, share_send, share_recv, tot_send, tot_recv, bank_send, bank_recv,
     ext_send, ext_recv, st_send, st_recv, ctx_send, ctx_recv,
 ):
     L = gate_ref.shape[1]
@@ -48,19 +50,49 @@
     score_scale = 4.0 * (C * CB) ** (-0.5)
     s, c = lax.axis_index("seq"), lax.axis_index("ch")
 
+    Y = C // 2
+    y, core = c // 2, lax.rem(c, 2)
+    sibling = c + 1 - 2 * core
+    pair = s + 1 - 2 * lax.rem(s, 2)
+    half_rows = B // 2
+    half_w = CB // 2
+
+    barrier = pltpu.get_barrier_semaphore()
+    for d in range(1, C):
+        pl.semaphore_signal(
+            barrier, inc=1, device_id=(s, lax.rem(c + d, C)), device_id_type=MESH
+        )
+    for d in range(1, S):
+        pl.semaphore_signal(
+            barrier, inc=1, device_id=(lax.rem(s + d, S), c), device_id_type=MESH
+        )
+
+    small = [
+        pltpu.make_async_copy(source, target, small_sem.at[i])
+        for i, (source, target) in enumerate(
+            ((gate_hbm, gate_ref), (mask_hbm, mask_ref), (neg_hbm, neg_ref), (gain_hbm, gain_ref))
+        )
+    ]
     own = [pltpu.make_async_copy(feat_hbm, feat_all.at[c, pl.ds(0, B)], local_sem.at[0])]
     for p in range(3):
         begin = pl.multiple_of(p * inner + c * W, 128)
         own.append(
             pltpu.make_async_copy(w_hbm.at[:, pl.ds(begin, W)], w_all.at[c, p], local_sem.at[1 + p])
         )
-    own.append(pltpu.make_async_copy(wpred_hbm, wpred, local_sem.at[4]))
-    for copy in own:
+    for copy in small + own:
         copy.start()
+    for copy in small:
+        copy.wait()
 
     aux_all[c, 0:HEADS] = gate_ref[...]
     base = (s * C + c) * L
     local_index = (neg_ref[...] - base).astype(jnp.float32)
+    diagonal = lax.broadcasted_iota(jnp.int32, (K, K), 0) == lax.broadcasted_iota(
+        jnp.int32, (K, K), 1
+    )
+    local_index = jnp.sum(
+        jnp.where(diagonal, jnp.broadcast_to(local_index, (K, K)), 0.0), axis=1, keepdims=True
+    )
     lead = jnp.where(
         lax.broadcasted_iota(jnp.int32, (HEADS, L), 0) == 0,
         jnp.broadcast_to(mask_ref[...].astype(jnp.float32), (HEADS, L)),
@@ -68,43 +100,89 @@
     )
     aux_all[c, HEADS:AUX_ROWS] = lead
     aux_all[c, NEG_ROW : NEG_ROW + K] = jnp.broadcast_to(local_index, (K, L))
-
-    barrier = pltpu.get_barrier_semaphore()
-    for d in range(1, C):
-        pl.semaphore_signal(
-            barrier, inc=1, device_id=(s, lax.rem(c + d, C)), device_id_type=MESH
-        )
-    for d in range(1, S):
-        pl.semaphore_signal(
-            barrier, inc=1, device_id=(lax.rem(s + d, S), c), device_id_type=MESH
-        )
     pl.semaphore_wait(barrier, S + C - 2)
 
-    def to_ch(d, kind):
-        peer = lax.rem(c + d, C)
-        if kind == 0:
-            source, target = aux_all.at[c], aux_all.at[c]
-        elif kind == 1:
-            source, target = feat_hbm, feat_all.at[c, pl.ds(0, B)]
-        else:
-            begin = pl.multiple_of((kind - 2) * inner + peer * W, 128)
-            source, target = w_hbm.at[:, pl.ds(begin, W)], w_all.at[c, kind - 2]
+    def remote(source, target, send, recv, device):
         return pltpu.make_async_remote_copy(
-            source, target, ch_send.at[d - 1, kind], ch_recv.at[d - 1, kind],
-            device_id=(s, peer), device_id_type=MESH,
+            source, target, send, recv, device_id=device, device_id_type=MESH
+        )
+
+    def to_ch(d):
+        return remote(
+            aux_all.at[c], aux_all.at[c], ch_send.at[d - 1], ch_recv.at[d - 1],
+            (s, lax.rem(c + d, C)),
+        )
+
+    def columns(p, peer):
+        return pl.ds(pl.multiple_of(p * inner + peer * W, 128), W)
+
+    def w_rows(block_s):
+        return pl.ds(pl.multiple_of(lax.rem(block_s, 2) * half_w, half_w), half_w)
+
+    def w_to_sibling(p):
+        return remote(
+            w_hbm.at[:, columns(p, sibling)], w_all.at[c, p],
+            w_send.at[0, p], w_recv.at[0, p], (s, sibling),
+        )
+
+    def features_to_sibling():
+        return remote(
+            feat_hbm, feat_all.at[c, pl.ds(0, B)], pass_send.at[0], pass_recv.at[0], (s, sibling)
+        )
+
+    def w_across(e, j, p):
+        peer = lax.rem(y + e, Y) * 2 + (core + j) % 2
+        n = 1 + 2 * (e - 1) + j
+        return remote(
+            w_hbm.at[w_rows(s), columns(p, peer)], w_all.at[c, p, w_rows(s)],
+            w_send.at[n, p], w_recv.at[n, p], (s, peer),
+        )
+
+    def features_across(e, j):
+        k = (core + j) % 2
+        rows = pl.ds(pl.multiple_of(k * half_rows, half_rows), half_rows)
+        n = 2 * (e - 1) + j
+        return remote(
+            feat_hbm.at[rows], feat_all.at[c, rows],
+            feat_send.at[n], feat_recv.at[n], (s, lax.rem(y + e, Y) * 2 + k),
+        )
+
+    def source(e, j):
+        return lax.rem(y + Y - e, Y) * 2 + (core + j) % 2
+
+    def pass_on(e, j, k):
+        block = lax.rem(y + Y - e, Y) * 2 + j
+        rows = pl.ds(pl.multiple_of(k * half_rows, half_rows), half_rows)
+        n = 1 + 2 * (e - 1) + j
+        return remote(
+            feat_all.at[block, rows], feat_all.at[block, rows],
+            pass_send.at[n], pass_recv.at[n], (s, sibling),
+        )
+
+    def share(e, j, p, block_s):
+        block = source(e, j)
+        n = 2 * (e - 1) + j
+        return remote(
+            w_all.at[block, p, w_rows(block_s)], w_all.at[block, p, w_rows(block_s)],
+            share_send.at[n, p], share_recv.at[n, p], (pair, c),
         )
 
     def to_seq(source, target, sends, recvs, d):
-        return pltpu.make_async_remote_copy(
-            source, target, sends.at[d - 1], recvs.at[d - 1],
-            device_id=(lax.rem(s + d, S), c), device_id_type=MESH,
-        )
-
-    sent = [to_ch(d, kind) for kind in range(5) for d in range(1, C)]
+        return remote(
+            source, target, sends.at[d - 1], recvs.at[d - 1], (lax.rem(s + d, S), c)
+        )
+
+    others = [(e, j) for e in range(1, Y) for j in range(2)]
+    sent = [to_ch(d) for d in range(1, C)]
+    sent += [w_across(e, j, p) for e, j in others for p in range(3)]
+    sent += [features_across(e, j) for e, j in others]
+    sent += [features_to_sibling()] + [w_to_sibling(p) for p in range(3)]
     for copy in sent:
         copy.start()
+    own_wpred = pltpu.make_async_copy(wpred_hbm, wpred, local_sem.at[4])
+    own_wpred.start()
     for d in range(1, C):
-        to_ch(d, 0).wait_recv()
+        to_ch(d).wait_recv()
 
     row_id = lax.broadcasted_iota(jnp.int32, (L, L), 0)
     column_id = lax.broadcasted_iota(jnp.int32, (L, L), 1)
@@ -129,9 +207,61 @@
     for copy in tot_copies:
         copy.start()
 
-    own[0].wait()
-    for d in range(1, C):
-        to_ch(d, 1).wait_recv()
+    def project(block, first=False, last=False):
+        for p in range(3):
+            part = dot(feat_all[block, 0:B, :], w_all[block, p])
+            if not first:
+                part = proj[p] + part
+            if last:
+                qkv[p] = part.astype(jnp.bfloat16)
+            else:
+                proj[p] = part
+
+    for copy in own:
+        copy.wait()
+    project(c, first=True)
+    for e, j in others:
+        for p in range(3):
+            w_across(e, j, p).wait_recv()
+            copy = share(e, j, p, s)
+            copy.start()
+            sent.append(copy)
+    features_to_sibling().wait_recv()
+    for p in range(3):
+        w_to_sibling(p).wait_recv()
+    project(sibling, last=Y == 1)
+    for e, j in others:
+        features_across(e, j).wait_recv()
+    for e, j in others:
+        copy = pass_on(e, j, core)
+        copy.start()
+        sent.append(copy)
+    for e, j in others:
+        pass_on(e, j, 1 - core).wait_recv()
+    for e, j in others:
+        for p in range(3):
+            share(e, j, p, pair).wait_recv()
+        project(source(e, j), last=(e, j) == others[-1])
+    eye = (row_id == column_id).astype(jnp.bfloat16)
+    for b in range(C):
+        keep = dot(eye, aux_all[b].astype(jnp.bfloat16), across)[:, MASK_ROW : MASK_ROW + 1]
+        rows = slice(b * L, (b + 1) * L)
+        qkv[2, rows, :] = (qkv[2, rows, :].astype(jnp.float32) * keep).astype(jnp.bfloat16)
+
+    for i in range(own_heads):
+        head = slice(i * HEAD_DIM, (i + 1) * HEAD_DIM)
+        tail = jnp.exp(cumcol[B - 1 : B, i : i + 1] - cumcol[:, i : i + 1])
+        high, low = split(qkv[1, :, head].astype(jnp.float32) * tail)
+        values = qkv[2, :, head]
+        state_out[head, :] = (dot(high, values, down) + dot(low, values, down)).astype(jnp.bfloat16)
+
+    def state_copy(d):
+        return to_seq(state_out, state_in.at[s], st_send, st_recv, d)
+
+    for d in reversed(range(1, S)):
+        @pl.when(s + d < S)
+        def _(d=d):
+            state_copy(d).start()
 
     wanted = jnp.concatenate([aux_all[b, NEG_ROW : NEG_ROW + K, :] for b in range(C)], axis=0)
     negatives = K * C
@@ -147,62 +277,29 @@
     for copy in bank_copies:
         copy.start()
 
-    def ext(kind):
+    def ext(kind, blocks):
         if kind == 0:
-            source, target = feat_all.at[:, pl.ds(0, 2 * L)], feat_all.at[:, pl.ds(B, 2 * L)]
+            source = feat_all.at[:, pl.ds(0, blocks * L)]
+            target = feat_all.at[:, pl.ds(B, blocks * L)]
         else:
             source, target = aux_all.at[pl.ds(0, 2)], aux_all.at[pl.ds(C, 2)]
-        return pltpu.make_async_remote_copy(
-            source, target, ext_send.at[kind], ext_recv.at[kind],
-            device_id=(lax.rem(s + S - 1, S), c), device_id_type=MESH,
-        )
-
-    reaching = c >= C - 2
-
-    @pl.when(reaching & (s > 0))
-    def _():
-        ext(0).start()
-        ext(1).start()
+        return remote(
+            source, target, ext_send.at[kind], ext_recv.at[kind], (lax.rem(s + S - 1, S), c)
+        )
+
+    def each_ext(condition, act):
+        for blocks in (1, 2):
+            @pl.when(condition & (c == C - 3 + blocks))
+            def _(blocks=blocks):
+                for kind in range(2):
+                    act(ext(kind, blocks))
+
+    each_ext(s > 0, lambda copy: copy.start())
 
     @pl.when(s == S - 1)
     def _():
         feat_all[:, B : B + 2 * L, :] = jnp.zeros((C, 2 * L, CB), jnp.bfloat16)
         aux_all[C : C + 2] = jnp.zeros((2, AUX_ROWS, 128), jnp.float32)
-
-    for d in range(C):
-        block = lax.rem(c + C - d, C)
-        for p in range(3):
-            if d == 0:
-                own[1 + p].wait()
-            else:
-                to_ch(d, 2 + p).wait_recv()
-            part = dot(feat_all[block, 0:B, :], w_all[block, p])
-            if d == 0:
-                proj[p] = part
-            elif d < C - 1:
-                proj[p] = proj[p] + part
-            else:
-                qkv[p] = (proj[p] + part).astype(jnp.bfloat16)
-    eye = (row_id == column_id).astype(jnp.bfloat16)
-    for b in range(C):
-        keep = dot(eye, aux_all[b].astype(jnp.bfloat16), across)[:, MASK_ROW : MASK_ROW + 1]
-        rows = slice(b * L, (b + 1) * L)
-        qkv[2, rows, :] = (qkv[2, rows, :].astype(jnp.float32) * keep).astype(jnp.bfloat16)
-
-    for i in range(own_heads):
-        head = slice(i * HEAD_DIM, (i + 1) * HEAD_DIM)
-        tail = jnp.exp(cumcol[B - 1 : B, i : i + 1] - cumcol[:, i : i + 1])
-        high, low = split(qkv[1, :, head].astype(jnp.float32) * tail)
-        values = qkv[2, :, head]
-        state_out[head, :] = (dot(high, values, down) + dot(low, values, down)).astype(jnp.bfloat16)
-
-    def state_copy(d):
-        return to_seq(state_out, state_in.at[s], st_send, st_recv, d)
-
-    for d in reversed(range(1, S)):
-        @pl.when(s + d < S)
-        def _(d=d):
-            state_copy(d).start()
 
     for i in range(own_heads):
         head = slice(i * HEAD_DIM, (i + 1) * HEAD_DIM)
@@ -264,14 +361,11 @@
     for d in range(1, C):
         to_owner(d).start()
     ctx_in[c] = ctx_out[c]
-    own[4].wait()
+    own_wpred.wait()
     for d in range(1, S):
         to_seq(bank.at[s], bank.at[s], bank_send, bank_recv, d).wait_recv()
 
-    @pl.when(reaching & (s < S - 1))
-    def _():
-        ext(0).wait_recv()
-        ext(1).wait_recv()
+    each_ext(s < S - 1, lambda copy: copy.wait_recv())
 
     for d in range(1, C):
         to_owner(d).wait_recv()
@@ -313,10 +407,7 @@
     for copy in sent + tot_copies + bank_copies:
         copy.wait_send()
 
-    @pl.when(reaching & (s > 0))
-    def _():
-        ext(0).wait_send()
-        ext(1).wait_send()
+    each_ext(s > 0, lambda copy: copy.wait_send())
 
     for d in range(1, S):
         @pl.when(s + d < S)
@@ -341,9 +432,13 @@
             jax.ShapeDtypeStruct((L, inner), bf16),
             jax.ShapeDtypeStruct((K, L), f32),
         ),
-        in_specs=[hbm, hbm, vmem, vmem, hbm, vmem, vmem],
+        in_specs=[hbm] * 7,
         out_specs=(vmem, vmem),
         scratch_shapes=[
+            pltpu.VMEM((HEADS, L), f32),
+            pltpu.VMEM((HEADS, HEAD_DIM), f32),
+            pltpu.VMEM((1, L), jnp.int32),
+            pltpu.VMEM((1, K), jnp.int32),
             pltpu.VMEM((C, B + 2 * L, CB), bf16),
             pltpu.VMEM((C, 3, CB, W), bf16),
             pltpu.VMEM((C + 2, AUX_ROWS, 128), f32),
@@ -360,9 +455,18 @@
             pltpu.VMEM((C, L, W), bf16),
             pltpu.VMEM((C, L, W), bf16),
             pltpu.VMEM(w_pred.shape, bf16),
+            dma((4,)),
             dma((5,)),
-            dma((C - 1, 5)),
-            dma((C - 1, 5)),
+            dma((C - 1,)),
+            dma((C - 1,)),
+            dma((C - 2,)),
+            dma((C - 2,)),
+            dma((C - 1,)),
+            dma((C - 1,)),
+            dma((C - 1, 3)),
+            dma((C - 1, 3)),
+            dma((C - 2, 3)),
+            dma((C - 2, 3)),
             dma((S - 1,)),
             dma((S - 1,)),
             dma((S - 1,)),
@@ -375,7 +479,7 @@
             dma((C - 1,)),
         ],
         compiler_params=pltpu.CompilerParams(
-            collective_id=0, has_side_effects=True, vmem_limit_bytes=48 * 2**20
+            collective_id=0, has_side_effects=True, vmem_limit_bytes=60 * 2**20
         ),
     )(
         features,
@@ -384,7 +488,7 @@
         norm_gain.reshape(HEADS, HEAD_DIM),
         w_pred,
         patch_mask.reshape(1, L),
-        neg_index,
+        neg_index.T,
     )
 
 

time: 62.4 us -> 49.9 us (0.80)
  Pallas kernels: 55.1 us -> 46.1 us
  local copies, waits for them, and re-layouts: 6.41 us -> 2.92 us
    pallas_call x1, Pallas kernels: 55.1 us -> 46.1 us  [shards(): pl.pallas_call(functools.partial(kernel, S, C), out_shape=(jax.ShapeDtype...]
    unnamed x13 -> x2, local copies, waits for them, and re-layouts: 6.41 us -> 2.92 us
where the time goes in v2:
time: 49.9 us; the launch traced here: 49.6 us
  Pallas kernels  46.1 us (92%)
  local copies, waits for them, and re-layouts  2.92 us (6%)
  between operations  0.64 us (1%)
    pallas_call x1, Pallas kernels, shards(): pl.pallas_call(functools.partial(kernel, S, C), out_shape=(jax.ShapeDtype...  46.1 us
    unnamed x2, local copies, waits for them, and re-layouts  2.92 us

profile of v2, /device:TPU:21, one launch (start us, length us, event | category | flops | bytes accessed | tf_op | source)
XLA Modules:
  0.0 49.6 jit_solution(12673604636664648605)
XLA Ops:
  0.6 46.1 %shard_map.86 = (bf16[128,1024]{1,0:T(8,128)(2,1)}, f32[4,128]{1,0:T(4,128)}) custom-call(bf16[512,256]{1,0:T(8,128)(2,1)} %feat_hbm.1, bf16[256,3072]{1,0:T(8,128)(2,1)} %w_hbm.1, f32[8,128]{1,0:T(8,128)} %gate_hbm.1, f32[8,128]{1,0:T(8,128)} %bitcast.3, bf16[4,1024,1024]{2,1,0:T(8,128)(2,1)} %wpred_hbm.1, s32[1,128]{1,0:T(1,128)} %bitcast.4, s32[1,4]{1,0:T(1,128)} %bitcast.5), custom_call_target="tpu_custom_call" | custom-call | tf_op jit(solution)/shard_map/pallas_call | solution.py:429
  46.7 1.7 %copy.11 = bf16[128,1024]{1,0:T(8,128)(2,1)} copy(bf16[128,1024]{1,0:T(8,128)(2,1)} %get-tuple-element.4) | data formatting | bytes 524288
  48.4 1.2 %copy.12 = f32[4,128]{1,0:T(4,128)} copy(f32[4,128]{1,0:T(4,128)} %get-tuple-element.5) | data formatting | bytes 4096

commit v3 on v2

--- a/solution.py
+++ b/solution.py
@@ -35,10 +35,10 @@
     ctx_ref, loss_ref,
     gate_ref, gain_ref, mask_ref, neg_ref,
     feat_all, w_all, aux_all, sel, totals, bank, proj, qkv, cumrow, cumcol,
-    state_out, state_in, carried, ctx_out, ctx_in, wpred,
+    state_out, pair_in, both, halves, gathered, before, carried, ctx_out, ctx_in, wpred,
     small_sem, local_sem, ch_send, ch_recv, feat_send, feat_recv, pass_send, pass_recv,
     w_send, w_recv, share_send, share_recv, tot_send, tot_recv, bank_send, bank_recv,
-    ext_send, ext_recv, st_send, st_recv, ctx_send, ctx_recv,
+    ext_send, ext_recv, pair_send, pair_recv, spread_send, spread_recv, st_send, st_recv, ctx_send, ctx_recv,
 ):
     L = gate_ref.shape[1]
     B = C * L
@@ -207,6 +207,22 @@
     for copy in tot_copies:
         copy.start()
 
+    wanted = jnp.concatenate([aux_all[b, NEG_ROW : NEG_ROW + K, :] for b in range(C)], axis=0)
+    negatives = K * C
+    owner = lax.broadcasted_iota(jnp.int32, (negatives, L), 0) // K
+    lane = lax.broadcasted_iota(jnp.int32, (negatives, L), 1).astype(jnp.float32)
+    hit = wanted == lane
+    chosen = jnp.concatenate(
+        [jnp.where(hit & (owner == b), 1.0, 0.0) for b in range(C)], axis=1
+    ).astype(jnp.bfloat16)
+    own[0].wait()
+    bank[c, s] = dot(chosen, feat_all[c, 0:B, :]).astype(jnp.bfloat16)
+    bank_copies = [
+        to_seq(bank.at[c, s], bank.at[c, s], bank_send, bank_recv, d) for d in range(1, S)
+    ]
+    for copy in bank_copies:
+        copy.start()
+
     def project(block, first=False, last=False):
         for p in range(3):
             part = dot(feat_all[block, 0:B, :], w_all[block, p])
@@ -217,7 +233,7 @@
             else:
                 proj[p] = part
 
-    for copy in own:
+    for copy in own[1:]:
         copy.wait()
     project(c, first=True)
     for e, j in others:
@@ -255,27 +271,8 @@
         values = qkv[2, :, head]
         state_out[head, :] = (dot(high, values, down) + dot(low, values, down)).astype(jnp.bfloat16)
 
-    def state_copy(d):
-        return to_seq(state_out, state_in.at[s], st_send, st_recv, d)
-
-    for d in reversed(range(1, S)):
-        @pl.when(s + d < S)
-        def _(d=d):
-            state_copy(d).start()
-
-    wanted = jnp.concatenate([aux_all[b, NEG_ROW : NEG_ROW + K, :] for b in range(C)], axis=0)
-    negatives = K * C
-    owner = lax.broadcasted_iota(jnp.int32, (negatives, L), 0) // K
-    lane = lax.broadcasted_iota(jnp.int32, (negatives, L), 1).astype(jnp.float32)
-    hit = wanted == lane
-    chosen = jnp.concatenate(
-        [jnp.where(hit & (owner == b), 1.0, 0.0) for b in range(C)], axis=1
-    ).astype(jnp.bfloat16)
-    for b in range(C):
-        bank[s, b] = dot(chosen, feat_all[b, 0:B, :]).astype(jnp.bfloat16)
-    bank_copies = [to_seq(bank.at[s], bank.at[s], bank_send, bank_recv, d) for d in range(1, S)]
-    for copy in bank_copies:
-        copy.start()
+    exchange = remote(state_out, pair_in, pair_send.at[0], pair_recv.at[0], (pair, c))
+    exchange.start()
 
     def ext(kind, blocks):
         if kind == 0:
@@ -300,6 +297,48 @@
     def _():
         feat_all[:, B : B + 2 * L, :] = jnp.zeros((C, 2 * L, CB), jnp.bfloat16)
         aux_all[C : C + 2] = jnp.zeros((2, AUX_ROWS, 128), jnp.float32)
+
+    for d in range(1, S):
+        to_seq(totals.at[s], totals.at[s], tot_send, tot_recv, d).wait_recv()
+    group, odd = s // 2, lax.rem(s, 2)
+    G = S // 2
+    half = W // 2
+    mine_half = pl.ds(pl.multiple_of(odd * half, half), half)
+    other_half = pl.ds(pl.multiple_of((1 - odd) * half, half), half)
+    part_rows = min(half, HEAD_DIM)
+    exchange.wait_recv()
+    is_odd = odd == 1
+    for i in range(own_heads):
+        head = slice(i * HEAD_DIM, (i + 1) * HEAD_DIM)
+        ours = state_out[head, :].astype(jnp.float32)
+        theirs = pair_in[head, :].astype(jnp.float32)
+        first = jnp.where(is_odd, theirs, ours)
+        second = jnp.where(is_odd, ours, theirs)
+        later = jnp.exp(totals[2 * group + 1, i : i + 1, :])
+        both[head, :] = (later * first + second).astype(jnp.bfloat16)
+
+    def half_copy(d):
+        return remote(
+            both.at[mine_half], halves.at[group], st_send.at[d - 1], st_recv.at[d - 1],
+            (lax.rem(s + 2 * d, S), c),
+        )
+
+    for d in reversed(range(1, G)):
+        @pl.when(group + d < G)
+        def _(d=d):
+            half_copy(d).start()
+
+    for d in range(1, S):
+        to_seq(bank.at[c, s], bank.at[c, s], bank_send, bank_recv, d).wait_recv()
+
+    def bank_to_ch(d):
+        return remote(
+            bank.at[c], bank.at[c], spread_send.at[d - 1], spread_recv.at[d - 1],
+            (s, lax.rem(c + d, C)),
+        )
+
+    for d in range(1, C):
+        bank_to_ch(d).start()
 
     for i in range(own_heads):
         head = slice(i * HEAD_DIM, (i + 1) * HEAD_DIM)
@@ -317,26 +356,41 @@
             values = qkv[2, 0:width, head]
             proj[0, rows, head] = dot(high, values) + dot(low, values)
 
-    for d in range(1, S):
-        to_seq(totals.at[s], totals.at[s], tot_send, tot_recv, d).wait_recv()
-    carried[...] = jnp.zeros_like(carried)
+    gathered[...] = jnp.zeros_like(gathered)
 
     def absorb(turn, _):
-        far = s - turn
-        pltpu.make_async_remote_copy(
-            state_out, state_in.at[turn], st_send.at[far - 1], st_recv.at[far - 1],
-            device_id=(lax.rem(s + 1, S), c), device_id_type=MESH,
+        far = group - turn
+        remote(
+            both.at[mine_half], halves.at[turn], st_send.at[far - 1], st_recv.at[far - 1],
+            (pair, c),
         ).wait_recv()
-        total = totals[turn]
-        for i in range(own_heads):
-            head = slice(i * HEAD_DIM, (i + 1) * HEAD_DIM)
-            carried[head, :] = (
-                jnp.exp(total[i : i + 1, :]) * carried[head, :]
-                + state_in[turn, head, :].astype(jnp.float32)
+        for n in range(half // part_rows):
+            rows = slice(n * part_rows, (n + 1) * part_rows)
+            h = (odd * half + n * part_rows) // HEAD_DIM
+            fade = jnp.exp(
+                totals[2 * turn, pl.ds(h, 1), :] + totals[2 * turn + 1, pl.ds(h, 1), :]
             )
+            gathered[rows, :] = fade * gathered[rows, :] + halves[turn, rows, :].astype(jnp.float32)
         return 0
 
-    lax.fori_loop(0, s, absorb, 0)
+    lax.fori_loop(0, group, absorb, 0)
+    before[mine_half, :] = gathered[...].astype(jnp.bfloat16)
+
+    swap = remote(
+        before.at[mine_half], before.at[mine_half], pair_send.at[1], pair_recv.at[1], (pair, c)
+    )
+    swapped = remote(
+        before.at[other_half], before.at[other_half], pair_send.at[1], pair_recv.at[1], (pair, c)
+    )
+    swap.start()
+    swapped.wait_recv()
+    for i in range(own_heads):
+        head = slice(i * HEAD_DIM, (i + 1) * HEAD_DIM)
+        start = before[head, :].astype(jnp.float32)
+        fade = jnp.exp(totals[2 * group, i : i + 1, :])
+        carried[head, :] = jnp.where(
+            is_odd, fade * start + pair_in[head, :].astype(jnp.float32), start
+        )
 
     for i in range(own_heads):
         head = slice(i * HEAD_DIM, (i + 1) * HEAD_DIM)
@@ -362,8 +416,8 @@
         to_owner(d).start()
     ctx_in[c] = ctx_out[c]
     own_wpred.wait()
-    for d in range(1, S):
-        to_seq(bank.at[s], bank.at[s], bank_send, bank_recv, d).wait_recv()
+    for d in range(1, C):
+        bank_to_ch(d).wait_recv()
 
     each_ext(s < S - 1, lambda copy: copy.wait_recv())
 
@@ -386,7 +440,7 @@
             part = predicted[:, b * CB : (b + 1) * CB]
             target = feat_all[b, pl.ds(begin, L), :]
             products = products + part.astype(jnp.float32) * target.astype(jnp.float32)
-            logits = logits + dot(part, bank[:, b].reshape(width, CB), across)
+            logits = logits + dot(part, bank[b].reshape(width, CB), across)
         positive = jnp.sum(products, axis=1, keepdims=True) * score_scale
         negsum = jnp.sum(
             jnp.where(mine == j, jnp.exp(logits * score_scale), 0.0), axis=1, keepdims=True
@@ -409,11 +463,14 @@
 
     each_ext(s > 0, lambda copy: copy.wait_send())
 
-    for d in range(1, S):
-        @pl.when(s + d < S)
+    exchange.wait_send()
+    swap.wait_send()
+    for d in range(1, G):
+        @pl.when(group + d < G)
         def _(d=d):
-            state_copy(d).wait_send()
-    for d in range(1, C):
+            half_copy(d).wait_send()
+    for d in range(1, C):
+        bank_to_ch(d).wait_send()
         to_owner(d).wait_send()
 
 
@@ -444,13 +501,17 @@
             pltpu.VMEM((C + 2, AUX_ROWS, 128), f32),
             pltpu.VMEM((C, 8, 128), f32),
             pltpu.VMEM((S, 8, 128), f32),
-            pltpu.VMEM((S, C, K * C, CB), bf16),
+            pltpu.VMEM((C, S, K * C, CB), bf16),
             pltpu.VMEM((3, B, W), f32),
             pltpu.VMEM((3, B, W), bf16),
             pltpu.VMEM((8, B), f32),
             pltpu.VMEM((B, 8), f32),
             pltpu.VMEM((W, HEAD_DIM), bf16),
-            pltpu.VMEM((S, W, HEAD_DIM), bf16),
+            pltpu.VMEM((W, HEAD_DIM), bf16),
+            pltpu.VMEM((W, HEAD_DIM), bf16),
+            pltpu.VMEM((S // 2, W // 2, HEAD_DIM), bf16),
+            pltpu.VMEM((W // 2, HEAD_DIM), f32),
+            pltpu.VMEM((W, HEAD_DIM), bf16),
             pltpu.VMEM((W, HEAD_DIM), f32),
             pltpu.VMEM((C, L, W), bf16),
             pltpu.VMEM((C, L, W), bf16),
@@ -473,8 +534,12 @@
             dma((S - 1,)),
             dma((2,)),
             dma((2,)),
-            dma((S - 1,)),
-            dma((S - 1,)),
+            dma((2,)),
+            dma((2,)),
+            dma((C - 1,)),
+            dma((C - 1,)),
+            dma((S // 2 - 1,)),
+            dma((S // 2 - 1,)),
             dma((C - 1,)),
             dma((C - 1,)),
         ],

time: 49.9 us -> 52.8 us (1.058)
  the two profiles are of different devices: /device:TPU:21 before, /device:TPU:9 now
where the time goes in v3:
time: 52.8 us; the launch traced here: 52.6 us
  Pallas kernels  49.1 us (93%)
  local copies, waits for them, and re-layouts  2.92 us (6%)
  between operations  0.64 us (1%)
    pallas_call x1, Pallas kernels, shards(): pl.pallas_call(functools.partial(kernel, S, C), out_shape=(jax.ShapeDtype...  49.1 us
    unnamed x2, local copies, waits for them, and re-layouts  2.92 us

profile of v3, /device:TPU:9, one launch (start us, length us, event | category | flops | bytes accessed | tf_op | source)
XLA Modules:
  0.0 52.6 jit_solution(386742009321671182)
XLA Ops:
  0.6 49.1 %shard_map.86 = (bf16[128,1024]{1,0:T(8,128)(2,1)}, f32[4,128]{1,0:T(4,128)}) custom-call(bf16[512,256]{1,0:T(8,128)(2,1)} %feat_hbm.1, bf16[256,3072]{1,0:T(8,128)(2,1)} %w_hbm.1, f32[8,128]{1,0:T(8,128)} %gate_hbm.1, f32[8,128]{1,0:T(8,128)} %bitcast.3, bf16[4,1024,1024]{2,1,0:T(8,128)(2,1)} %wpred_hbm.1, s32[1,128]{1,0:T(1,128)} %bitcast.4, s32[1,4]{1,0:T(1,128)} %bitcast.5), custom_call_target="tpu_custom_call" | custom-call | tf_op jit(solution)/shard_map/pallas_call | solution.py:486
  49.7 1.7 %copy.11 = bf16[128,1024]{1,0:T(8,128)(2,1)} copy(bf16[128,1024]{1,0:T(8,128)(2,1)} %get-tuple-element.4) | data formatting | bytes 524288
  51.4 1.2 %copy.12 = f32[4,128]{1,0:T(4,128)} copy(f32[4,128]{1,0:T(4,128)} %get-tuple-element.5) | data formatting | bytes 4096
